TPU v7x, 256 devices: a whole 4x4x8 slice. The times are simulated.
256 devices in a mesh: chaos: 2 (over x_hi), azim: 32 (over z, y), axial: 4 (over x_lo, core).
Axes of the slice: x: 4 (x_hi: 2, x_lo: 2; x = x_hi * 2 + x_lo), y: 4, z: 8, core: 2. Of those that a mesh axis runs over, the one named last changes fastest.
Arguments:
- displacement: float32 [36, 3, 128, 128, 128], P('chaos', None, 'axial', 'azim'), may hold values from -6 to 6
- mean_modulus: float32 [128, 128, 128], P('axial', 'azim'), may hold values from 0.5 to 2
- kl_fields: float32 [7, 128, 128, 128], P(None, 'axial', 'azim'), may hold values from -4 to 4
- triple_cols: int32 [8, 36, 4], replicated, may hold values from 0 to 35, as said below
- triple_vals: float32 [8, 36, 4], replicated, may hold values from -1.5 to 1.5
Outputs:
- response: float32 [36, 3, 128, 128, 128], P('chaos', None, 'axial', 'azim')
Inputs may be any that keep to these rules, and one draw needn't show every extreme that they name: `triple_cols`: the 4 entries of one row are distinct; for expansion term 0 the first entry of row i is i.
All inputs are finite; a program needn't handle non-finite values.
Results may differ from a plain program's by a relative error of at most 0.0001.
Values sent between devices are 32-bit elements; how exact they have to be, the bound alone decides.
A program may use at most 192 MiB of HBM per device.

v0:
```python
import jax
import jax.numpy as jnp
from jax import lax
from jax.sharding import PartitionSpec as P


def extended(block, sides, width, periodic):
    for axis, dim in sides:
        count = lax.axis_size(axis)
        forward = [(i, i + 1) for i in range(count - 1)]
        if periodic:
            forward.append((count - 1, 0))
        backward = [(target, source) for source, target in forward]
        low = lax.ppermute(
            lax.slice_in_dim(block, block.shape[dim] - width, None, axis=dim), axis, forward
        )
        high = lax.ppermute(lax.slice_in_dim(block, 0, width, axis=dim), axis, backward)
        block = jnp.concatenate([low, block, high], axis=dim)
    return block


def coupling(slot_cols, slot_vals):
    modes = jnp.arange(slot_vals.shape[1], dtype=jnp.int32)
    matches = (slot_cols[..., None] == modes).astype(slot_vals.dtype)
    return jnp.sum(slot_vals[..., None] * matches, axis=2)


def lame_mix(dif_axial, dif_azim, dif_radial):
    component = jnp.arange(3, dtype=jnp.int32)[None, :, None, None, None]
    weight_axial = 1.0 + 2.0 * (component == 0).astype(dif_axial.dtype)
    weight_azim = 1.0 + 2.0 * (component == 1).astype(dif_axial.dtype)
    weight_radial = 1.0 + 2.0 * (component == 2).astype(dif_axial.dtype)
    return weight_axial * dif_axial + weight_azim * dif_azim + weight_radial * dif_radial


def stiffness(values):
    along_azim = extended(values, (("azim", 3),), 1, True)
    along_axial = extended(values, (("axial", 2),), 1, False)
    radial_pad = jnp.pad(values, ((0, 0), (0, 0), (0, 0), (0, 0), (1, 1)))
    dif_axial = 2.0 * values - along_axial[:, :, 2:] - along_axial[:, :, :-2]
    dif_azim = 2.0 * values - along_azim[:, :, :, 2:] - along_azim[:, :, :, :-2]
    dif_radial = 2.0 * values - radial_pad[..., 2:] - radial_pad[..., :-2]
    return lame_mix(dif_axial, dif_azim, dif_radial)


def combine(matrices, stiffened, fields):
    running = None
    for which in range(matrices.shape[0]):
        product_part = jnp.einsum(
            "ij,jcazr->icazr", matrices[which], stiffened, precision=lax.Precision.HIGHEST
        )
        scaled = fields[which][None, None] * product_part
        running = scaled if running is None else running + scaled
    return running


def on_device(displacement, mean_modulus, kl_fields, triple_cols, triple_vals):
    couple = coupling(triple_cols, triple_vals)
    fields = jnp.concatenate([mean_modulus[None], kl_fields], 0)
    mode_share = displacement.shape[0]
    first_mode = lax.axis_index("chaos") * mode_share
    gathered = lax.all_gather(displacement, "chaos", axis=0, tiled=True)
    stiffened = stiffness(gathered)
    matrices = lax.dynamic_slice_in_dim(couple, first_mode, mode_share, 1)
    return combine(matrices, stiffened, fields)


def solution(mesh):
    return jax.shard_map(
        on_device,
        mesh=mesh,
        in_specs=(
            P("chaos", None, "axial", "azim", None),
            P("axial", "azim", None),
            P(None, "axial", "azim", None),
            P(),
            P(),
        ),
        out_specs=P("chaos", None, "axial", "azim", None),
        check_vma=False,
    )
```

profile of v0, /device:TPU:1, one launch (start us, length us, event | category | flops | bytes accessed | tf_op | source)
XLA Modules:
  0.0 305.4 jit_solution(13578120863311177548)
XLA Ops:
  6.5 0.0 all-gather.2.cloned.1.call-start
  6.5 4.2 %copy.32 = f32[18,3,32,4,128]{4,2,3,1,0:T(8,128)} copy(f32[18,3,32,4,128]{4,3,2,1,0:T(4,128)} %param.5) | data formatting | bytes 7077888 | tf_op args[0]
  10.8 0.0 copy-start.7
  10.8 0.0 all-gather.2.cloned.1.call-update
  10.8 99.8 %all-gather.2.cloned.1.call-done = f32[36,3,32,4,128]{4,2,3,1,0:T(8,128)} async-done(((f32[18,3,32,4,128]{4,2,3,1,0:T(8,128)}), f32[36,3,32,4,128]{4,2,3,1,0:T(8,128)}) %all-gather.2.cloned.1.call-update) | async-done | bytes 7077904 | tf_op jit(solution)/shard_map/all_gather | solution.py:62
  110.6 4.3 %fusion.32 = (f32[36,3,32,1,128]{4,2,3,1,0:T(8,128)}, f32[36,3,32,1,128]{4,2,3,1,0:T(8,128)}) fusion(f32[36,3,32,4,128]{4,2,3,1,0:T(8,128)} %all-gather.2.cloned.1.call-done), kind=kLoop, calls=%fused_computation.66 | loop fusion | bytes 7077888 | tf_op jit(solution)/shard_map/slice | solution.py:17
  114.9 5.2 %collective-permute-start.2 = (f32[36,3,32,1,128]{4,2,3,1,0:T(8,128)}, f32[36,3,32,1,128]{4,2,3,1,0:T(8,128)S(1)}, u32[]{:S(2)}, u32[]{:S(2)}) collective-permute-start(f32[36,3,32,1,128]{4,2,3,1,0:T(8,128)} %get-tuple-element.7), channel_id=1, source_target_pairs={{4,0},{8,4},{12,8},{16,12},{20,16},{24,20},{28,24},{32,28},{36,32}... | collective-permute-start | bytes 5308424 | tf_op jit(solution)/shard_map/ppermute | solution.py:17
  120.1 0.0 collective-permute-start.3
  120.1 0.0 copy-done.7
  120.1 0.7 copy.29
  120.8 1.5 copy.30
  122.3 1.3 select_reduce_fusion
  123.6 0.1 constant_dynamic-slice_fusion.7
  123.7 2.5 fusion.31
  126.1 2.9 collective-permute-start
  129.0 2.7 collective-permute-start.1
  131.7 1.8 slice_bitcast_fusion.6
  133.5 0.1 collective-permute-done
  133.7 0.9 collective-permute-done.1
  134.6 23.1 %collective-permute-done.2 = f32[36,3,32,1,128]{4,2,3,1,0:T(8,128)S(1)} collective-permute-done((f32[36,3,32,1,128]{4,2,3,1,0:T(8,128)}, f32[36,3,32,1,128]{4,2,3,1,0:T(8,128)S(1)}, u32[]{:S(2)}, u32[]{:S(2)}) %collective-permute-start.2) | collective-permute-done | bytes 1769504 | tf_op jit(solution)/shard_map/ppermute | solution.py:17
  157.7 5.1 %collective-permute-done.3 = f32[36,3,32,1,128]{4,2,3,1,0:T(8,128)S(1)} collective-permute-done((f32[36,3,32,1,128]{4,2,3,1,0:T(8,128)}, f32[36,3,32,1,128]{4,2,3,1,0:T(8,128)S(1)}, u32[]{:S(2)}, u32[]{:S(2)}) %collective-permute-start.3) | collective-permute-done | bytes 1769504 | tf_op jit(solution)/shard_map/ppermute | solution.py:14
  162.8 17.2 %fusion.19 = f32[36,3,32,4,128]{4,2,3,1,0:T(8,128)S(1)} fusion(f32[36,3,32,4,128]{4,2,3,1,0:T(8,128)} %all-gather.2.cloned.1.call-done, f32[36,3,32,1,128]{4,2,3,1,0:T(8,128)S(1)} %collective-permute-done.3, f32[36,3,32,1,128]{4,2,3,1,0:T(8,128)S(1)} %collective-permute-done.2, f32[36,3,1,4,128]{4,2,3,1,0:T(1,128)S(1)} %collective-permute-done.1, ...), kind=kLoop, calls=%fused_computation.21 | loop fusion | flops 28311552 | bytes 18137124 | tf_op jit(solution)/shard_map/add | solution.py:33
  180.0 0.0 copy-start
  180.0 11.4 %fusion.10 = f32[18,3,32,4,128]{4,0,3,2,1:T(8,128)S(1)} fusion(f32[36,3,32,4,128]{4,2,3,1,0:T(8,128)S(1)} %fusion.19, f32[1,18,36]{2,0,1:T(1,128)S(1)} %get-tuple-element.21), kind=kOutput, calls=%fused_computation.12 | convolution fusion | flops 382205952 | bytes 10619424 | tf_op jit(solution)/shard_map/ij,jcazr->icazr/dot_general | solution.py:49
  191.4 13.5 %fusion.12 = f32[18,3,32,4,128]{4,0,3,2,1:T(8,128)} fusion(f32[36,3,32,4,128]{4,2,3,1,0:T(8,128)S(1)} %fusion.19, f32[1,18,36]{2,0,1:T(1,128)S(1)} %get-tuple-element.22), kind=kOutput, calls=%fused_computation.14 | convolution fusion | flops 382205952 | bytes 10619424 | tf_op jit(solution)/shard_map/ij,jcazr->icazr/dot_general | solution.py:49
  204.9 13.5 %fusion.14 = f32[18,3,32,4,128]{4,0,3,2,1:T(8,128)} fusion(f32[36,3,32,4,128]{4,2,3,1,0:T(8,128)S(1)} %fusion.19, f32[1,18,36]{2,0,1:T(1,128)S(1)} %get-tuple-element.23), kind=kOutput, calls=%fused_computation.16 | convolution fusion | flops 382205952 | bytes 10619424 | tf_op jit(solution)/shard_map/ij,jcazr->icazr/dot_general | solution.py:49
  218.4 13.5 %fusion.4 = f32[18,3,32,4,128]{4,0,3,2,1:T(8,128)} fusion(f32[36,3,32,4,128]{4,2,3,1,0:T(8,128)S(1)} %fusion.19, f32[1,18,36]{2,0,1:T(1,128)S(1)} %get-tuple-element.18), kind=kOutput, calls=%fused_computation.6 | convolution fusion | flops 382205952 | bytes 10619424 | tf_op jit(solution)/shard_map/ij,jcazr->icazr/dot_general | solution.py:49
  231.9 13.7 %fusion.6 = f32[18,3,32,4,128]{4,0,3,2,1:T(8,128)} fusion(f32[36,3,32,4,128]{4,2,3,1,0:T(8,128)S(1)} %fusion.19, f32[1,18,36]{2,0,1:T(1,128)S(1)} %get-tuple-element.19), kind=kOutput, calls=%fused_computation.8 | convolution fusion | flops 382205952 | bytes 10619424 | tf_op jit(solution)/shard_map/ij,jcazr->icazr/dot_general | solution.py:49
  245.6 13.4 %fusion.8 = f32[18,3,32,4,128]{4,0,3,2,1:T(8,128)} fusion(f32[36,3,32,4,128]{4,2,3,1,0:T(8,128)S(1)} %fusion.19, f32[1,18,36]{2,0,1:T(1,128)S(1)} %get-tuple-element.20), kind=kOutput, calls=%fused_computation.10 | convolution fusion | flops 382205952 | bytes 10619424 | tf_op jit(solution)/shard_map/ij,jcazr->icazr/dot_general | solution.py:49
  259.0 0.0 copy-start.1
  259.0 0.0 copy-start.2
  259.0 0.0 copy-start.3
  259.0 0.0 copy-start.4
  259.0 0.0 copy-start.5
  259.0 0.0 copy-start.6
  259.0 0.0 copy-done
  259.0 13.4 %fusion.2 = f32[18,3,32,4,128]{4,0,3,2,1:T(8,128)} fusion(f32[36,3,32,4,128]{4,2,3,1,0:T(8,128)S(1)} %fusion.19, f32[1,18,36]{2,0,1:T(1,128)S(1)} %get-tuple-element.17), kind=kOutput, calls=%fused_computation.4 | convolution fusion | flops 382205952 | bytes 10619424 | tf_op jit(solution)/shard_map/ij,jcazr->icazr/dot_general | solution.py:49
  272.5 0.0 copy-done.1
  272.5 0.0 copy-done.2
  272.5 0.0 copy-done.3
  272.5 0.0 copy-done.4
  272.5 0.0 copy-done.5
  272.5 0.0 copy-done.6
  272.5 20.7 %multiply_add_fusion = f32[18,3,32,4,128]{4,0,3,2,1:T(8,128)} fusion(f32[18,3,32,4,128]{4,0,3,2,1:T(8,128)} %fusion.2, f32[18,3,32,4,128]{4,0,3,2,1:T(8,128)} %fusion.4, f32[18,3,32,4,128]{4,0,3,2,1:T(8,128)} %fusion.6, f32[18,3,32,4,128]{4,0,3,2,1:T(8,128)} %fusion.8, f32[18,3,32,4,128]{4,0,3,2,1:T(8,128)S(1)} %fusion.10, ...), kind=kOutput, calls=%fused_computation.33 | convolution fusion | flops 395476992 | bytes 35916320 | tf_op jit(solution)/shard_map/ij,jcazr->icazr/dot_general | solution.py:49
  293.2 5.0 %copy.41 = f32[18,3,32,4,128]{4,3,2,1,0:T(4,128)} copy(f32[18,3,32,4,128]{4,0,3,2,1:T(8,128)} %multiply_add_fusion) | data formatting | bytes 7077888 | tf_op jit(solution)/shard_map/add | solution.py:53
  (2 shorter events, 0.0 us)
Async XLA Ops:
  6.5 104.0 %all-gather.2.cloned.1.call-start = ((), (), s32[]{:S(2)}) async-start(), calls=%async_computation | async-start | bytes 10616832 | tf_op jit(solution)/shard_map/all_gather | solution.py:62
  10.8 109.3 %copy-start.7 = (s32[8,36,4]{1,2,0:T(4,128)S(1)}, s32[8,36,4]{1,2,0:T(4,128)}, u32[]{:S(2)}) copy-start(s32[8,36,4]{1,2,0:T(4,128)} %param.8) | copy-start | bytes 13828
  114.9 42.8 %collective-permute-start.2 = (f32[36,3,32,1,128]{4,2,3,1,0:T(8,128)}, f32[36,3,32,1,128]{4,2,3,1,0:T(8,128)S(1)}, u32[]{:S(2)}, u32[]{:S(2)}) collective-permute-start(f32[36,3,32,1,128]{4,2,3,1,0:T(8,128)} %get-tuple-element.7), channel_id=1, source_target_pairs={{4,0},{8,4},{12,8},{16,12},{20,16},{24,20},{28,24},{32,28},{36,32}... | collective-permute-start | bytes 5308424 | tf_op jit(solution)/shard_map/ppermute | solution.py:17
  120.1 42.7 %collective-permute-start.3 = (f32[36,3,32,1,128]{4,2,3,1,0:T(8,128)}, f32[36,3,32,1,128]{4,2,3,1,0:T(8,128)S(1)}, u32[]{:S(2)}, u32[]{:S(2)}) collective-permute-start(f32[36,3,32,1,128]{4,2,3,1,0:T(8,128)} %get-tuple-element.8), channel_id=1, source_target_pairs={{0,4},{4,8},{8,12},{12,16},{16,20},{20,24},{24,28},{28,32},{32,36}... | collective-permute-start | bytes 5308424 | tf_op jit(solution)/shard_map/ppermute | solution.py:14
  126.1 7.5 %collective-permute-start = (f32[36,3,1,4,128]{4,2,3,1,0:T(1,128)S(1)}, f32[36,3,1,4,128]{4,2,3,1,0:T(1,128)S(1)}, u32[]{:S(2)}, u32[]{:S(2)}) collective-permute-start(f32[36,3,1,4,128]{4,2,3,1,0:T(1,128)S(1)} %get-tuple-element.5), channel_id=1, source_target_pairs={{1,0},{2,1},{3,2},{5,4},{6,5},{7,6},{9,8},{10,9},{11,10},{13,12},{... | collective-permute-start | bytes 663560 | tf_op jit(solution)/shard_map/ppermute | solution.py:17
  129.0 5.6 %collective-permute-start.1 = (f32[36,3,1,4,128]{4,2,3,1,0:T(1,128)S(1)}, f32[36,3,1,4,128]{4,2,3,1,0:T(1,128)S(1)}, u32[]{:S(2)}, u32[]{:S(2)}) collective-permute-start(f32[36,3,1,4,128]{4,2,3,1,0:T(1,128)S(1)} %get-tuple-element.6), channel_id=1, source_target_pairs={{0,1},{1,2},{2,3},{4,5},{5,6},{6,7},{8,9},{9,10},{10,11},{12,13},{... | collective-permute-start | bytes 663560 | tf_op jit(solution)/shard_map/ppermute | solution.py:14
  180.0 79.0 %copy-start = (f32[36,3,32,4,128]{4,2,3,1,0:T(8,128)}, f32[36,3,32,4,128]{4,2,3,1,0:T(8,128)S(1)}, u32[]{:S(2)}) copy-start(f32[36,3,32,4,128]{4,2,3,1,0:T(8,128)S(1)} %fusion.19) | copy-start | bytes 21233668
  259.0 13.5 %copy-start.1 = (f32[32,4,128]{2,1,0:T(4,128)S(1)}, f32[32,4,128]{2,1,0:T(4,128)}, u32[]{:S(2)}) copy-start(f32[32,4,128]{2,1,0:T(4,128)} %get-tuple-element.9) | copy-start | bytes 196612
  259.0 13.5 %copy-start.2 = (f32[32,4,128]{2,1,0:T(4,128)S(1)}, f32[32,4,128]{2,1,0:T(4,128)}, u32[]{:S(2)}) copy-start(f32[32,4,128]{2,1,0:T(4,128)} %get-tuple-element.10) | copy-start | bytes 196612
  259.0 13.5 %copy-start.3 = (f32[32,4,128]{2,1,0:T(4,128)S(1)}, f32[32,4,128]{2,1,0:T(4,128)}, u32[]{:S(2)}) copy-start(f32[32,4,128]{2,1,0:T(4,128)} %get-tuple-element.11) | copy-start | bytes 196612
  259.0 13.5 %copy-start.4 = (f32[32,4,128]{2,1,0:T(4,128)S(1)}, f32[32,4,128]{2,1,0:T(4,128)}, u32[]{:S(2)}) copy-start(f32[32,4,128]{2,1,0:T(4,128)} %get-tuple-element.12) | copy-start | bytes 196612
  259.0 13.5 %copy-start.5 = (f32[32,4,128]{2,1,0:T(4,128)S(1)}, f32[32,4,128]{2,1,0:T(4,128)}, u32[]{:S(2)}) copy-start(f32[32,4,128]{2,1,0:T(4,128)} %get-tuple-element.13) | copy-start | bytes 196612
  259.0 13.5 %copy-start.6 = (f32[32,4,128]{2,1,0:T(4,128)S(1)}, f32[32,4,128]{2,1,0:T(4,128)}, u32[]{:S(2)}) copy-start(f32[32,4,128]{2,1,0:T(4,128)} %get-tuple-element.14) | copy-start | bytes 196612
Sparse Core Ops, SparseCore 0:
  10.9 99.6 all-gather.1
where the time goes:
time: 310 us; the launch traced here: 305 us
  waiting for transfers between devices  129 us (42%)
  matrix products  113 us (36%)
  local copies, waits for them, and re-layouts  20.2 us (7%)
  other arithmetic  18.5 us (6%)
  between operations  13.8 us (4%)
  starting transfers between devices  10.8 us (3%)
    dot_general x8, matrix products, combine(): jnp.einsum('ij,jcazr->icazr', matrices[which], stiffened, precision=lax.P...  113 us
    all_gather x1, waiting for transfers between devices, on_device(): gathered = lax.all_gather(displacement, 'chaos', axis=0, tiled=True)  99.8 us
    ppermute x2, waiting for transfers between devices, extended(): lax.ppermute(lax.slice_in_dim(block, 0, width, axis=dim), axis, backward)  23.2 us
    add x1, other arithmetic, lame_mix(): weight_axial * dif_axial + weight_azim * dif_azim  17.2 us
    ppermute x2, starting transfers between devices, extended(): lax.ppermute(lax.slice_in_dim(block, 0, width, axis=dim), axis, backward)  8.07 us
    slice x2, local copies, waits for them, and re-layouts, extended(): lax.slice_in_dim(block, 0, width, axis=dim)  6.74 us
    unnamed x19, local copies, waits for them, and re-layouts  6.48 us
  transfers between devices with their start and end apart: 5, of which 5 were waited for; matrix products, arithmetic and copies ran while one was open for 3% of the time, Pallas kernels for 0%

commit v1 on v0

v1 whole, which is shorter than its diff:
```python
import functools

import jax
import jax.numpy as jnp
from jax import lax
from jax.experimental import pallas as pl
from jax.experimental.pallas import tpu as pltpu
from jax.sharding import PartitionSpec as P

MESH = pl.DeviceIdType.MESH
F32 = jnp.float32
PAD = 8
IN_FLIGHT = 3


def place_of(group, place):
    if group == 0:
        return 1 + place // 2, 1 + place % 2
    if group == 1:
        return 1 + place // 2, 3 * (place % 2)
    return 3 * (place % 2), 2 * (group - 2) + place // 2


def kernel(
    shape,
    u_hbm, mean_hbm, kl_hbm, cols, vals, out_hbm,
    u, fields, azim_send, azim_recv, axial_send, axial_recv, stiff, work, out,
    load_sem, store_sem, azim_ssem, azim_rsem, axial_ssem, axial_rsem, send_sem, recv_sem,
):
    modes, comps, axials, azims, terms, slots = shape
    rows = axials * azims
    vectors = modes * comps
    chaos = lax.axis_index("chaos")
    azim = lax.axis_index("azim")
    axial = lax.axis_index("axial")
    n_azim, n_axial = lax.axis_size("azim"), lax.axis_size("axial")
    partner = {"chaos": 1 - chaos}
    azim_next = {"azim": lax.rem(azim + 1, n_azim)}
    azim_prev = {"azim": lax.rem(azim + n_azim - 1, n_azim)}
    axial_next = {"axial": lax.rem(axial + 1, n_axial)}
    axial_prev = {"axial": lax.rem(axial + n_axial - 1, n_axial)}
    has_prev, has_next = axial > 0, axial < n_axial - 1

    load_u = pltpu.make_async_copy(u_hbm, u.at[:, pl.ds(PAD, rows)], load_sem.at[0])
    load_mean = pltpu.make_async_copy(mean_hbm, fields.at[pl.ds(0, 1)], load_sem.at[1])
    load_kl = pltpu.make_async_copy(kl_hbm, fields.at[pl.ds(1, terms - 1)], load_sem.at[2])
    load_u.start()
    load_mean.start()
    load_kl.start()

    barrier = pltpu.get_barrier_semaphore()
    for target in (partner, azim_next, azim_prev, axial_next, axial_prev):
        pl.semaphore_signal(barrier, inc=1, device_id=target, device_id_type=MESH)

    def remote(source, target, ssem, rsem, device):
        return pltpu.make_async_remote_copy(
            src_ref=source, dst_ref=target, send_sem=ssem, recv_sem=rsem,
            device_id=device, device_id_type=MESH,
        )

    axial_copies = [
        remote(axial_send.at[s], axial_recv.at[s], axial_ssem.at[s], axial_rsem.at[s], d)
        for s, d in ((0, axial_prev), (1, axial_next))
    ]
    azim_copies = [
        remote(azim_send.at[s], azim_recv.at[s], azim_ssem.at[s], azim_rsem.at[s], d)
        for s, d in ((0, azim_prev), (1, azim_next))
    ]

    own = pl.ds(chaos * vectors, vectors)

    def exchange(n):
        part = stiff.at[n, own]
        return remote(part, part, send_sem.at[n], recv_sem.at[n], partner)

    load_u.wait()

    def pack_axial(p, carry):
        for s, first in ((0, PAD), (1, PAD + rows - azims)):
            axial_send[s, p, 0:azims, :] = u[2 * p, first:first + azims, :]
            axial_send[s, p, azims:2 * azims, :] = u[2 * p + 1, first:first + azims, :]
        return carry

    lax.fori_loop(0, vectors // 2, pack_axial, 0)
    pl.semaphore_wait(barrier, 5)

    @pl.when(has_prev)
    def _():
        axial_copies[0].start()

    @pl.when(has_next)
    def _():
        axial_copies[1].start()

    lane = lax.broadcasted_iota(jnp.int32, (8, 128), 1)
    first_lane, last_lane = lane == 0, lane == 127

    def stencil(group):
        where = [place_of(group, place) for place in range(4)]

        def body(j, carry):
            for c in range(comps):
                v = j * comps + c
                for place, (z, at) in enumerate(where):
                    base = PAD + at * 8 * azims + z

                    def layer(shift):
                        return u[v, pl.ds(base + shift, 8, stride=azims), :]

                    x = layer(0)
                    low = layer(-1) if z > 0 else azim_recv[1, v, at * 8:at * 8 + 8, :]
                    high = layer(1) if z < azims - 1 else azim_recv[0, v, at * 8:at * 8 + 8, :]
                    pairs = [
                        layer(azims) + layer(-azims),
                        low + high,
                        jnp.where(first_lane, 0.0, pltpu.roll(x, 1, 1))
                        + jnp.where(last_lane, 0.0, pltpu.roll(x, 127, 1)),
                    ]
                    total = pairs[(c + 1) % 3] + pairs[(c + 2) % 3] + 3.0 * pairs[c]
                    stiff[4 * group + place, chaos * vectors + v] = 10.0 * x - total
            return carry

        lax.fori_loop(0, modes, body, 0)

    def couple(group):
        def body(place, carry):
            n = 4 * group + place
            exchange(n).wait_recv()
            z, at = place_of(group, place)
            start = at * (8 * azims) + z
            blocks = pl.ds(start, 8, stride=azims)

            def gather(v, carry):
                work[v] = stiff[n, v]
                return carry

            lax.fori_loop(0, 2 * vectors, gather, 0, unroll=12)
            factors = [fields[k, blocks, :] for k in range(terms)]

            def row(i, carry):
                mode = chaos * modes + i
                total = [jnp.zeros((8, 128), F32) for c in range(comps)]
                for k in range(terms):
                    part = [None] * comps
                    for s in range(slots):
                        column, value = cols[k, s, mode] * comps, vals[k, s, mode]
                        for c in range(comps):
                            term = value * work[column + c]
                            part[c] = term if s == 0 else part[c] + term
                    for c in range(comps):
                        total[c] = total[c] + factors[k] * part[c]
                for c in range(comps):
                    out[i * comps + c, blocks, :] = total[c]
                return carry

            lax.fori_loop(0, modes, row, 0)
            exchange(n).wait_send()
            if group < 3:
                exchange(n + IN_FLIGHT).start()
            else:
                @pl.when(n + IN_FLIGHT < 16)
                def _():
                    exchange(n + IN_FLIGHT).start()

            return carry

        lax.fori_loop(0, 4, body, 0)

    def store(at):
        part = pl.ds(at * 8 * azims, 8 * azims)
        return pltpu.make_async_copy(out.at[:, part], out_hbm.at[:, part], store_sem.at[at])

    stencil(0)
    for n in range(IN_FLIGHT):
        exchange(n).start()

    def pack_azim(v, carry):
        for at in range(axials // 8):
            for s, z in ((0, 0), (1, azims - 1)):
                azim_send[s, v, at * 8:at * 8 + 8, :] = u[
                    v, pl.ds(PAD + at * 8 * azims + z, 8, stride=azims), :]
        return carry

    lax.fori_loop(0, vectors, pack_azim, 0, unroll=2)
    for copy in azim_copies:
        copy.start()

    for has, s, first in ((has_prev, 1, PAD - azims), (has_next, 0, PAD + rows)):
        @pl.when(has)
        def _(s=s, first=first):
            axial_copies[s].wait_recv()

            def unpack(p, carry):
                u[2 * p, first:first + azims, :] = axial_recv[s, p, 0:azims, :]
                u[2 * p + 1, first:first + azims, :] = axial_recv[s, p, azims:2 * azims, :]
                return carry

            lax.fori_loop(0, vectors // 2, unpack, 0)

        @pl.when(jnp.logical_not(has))
        def _(first=first):
            def clear(v, carry):
                u[v, first:first + azims, :] = jnp.zeros((azims, 128), F32)
                return carry

            lax.fori_loop(0, vectors, clear, 0)

    stencil(1)
    load_mean.wait()
    load_kl.wait()
    couple(0)
    for copy in azim_copies:
        copy.wait_recv()
    stencil(2)
    stencil(3)
    couple(1)
    couple(2)
    store(0).start()
    store(1).start()
    couple(3)
    store(2).start()
    store(3).start()

    @pl.when(has_prev)
    def _():
        axial_copies[0].wait_send()

    @pl.when(has_next)
    def _():
        axial_copies[1].wait_send()

    for copy in azim_copies:
        copy.wait_send()
    for at in range(4):
        store(at).wait()


def on_device(displacement, mean_modulus, kl_fields, triple_cols, triple_vals):
    modes, comps, axials, azims, radials = displacement.shape
    terms, all_modes, slots = triple_cols.shape
    vectors, rows = modes * comps, axials * azims
    dma = pltpu.SemaphoreType.DMA
    anywhere = pl.BlockSpec(memory_space=pl.ANY)
    scalar = pl.BlockSpec(memory_space=pltpu.SMEM)
    result = pl.pallas_call(
        functools.partial(kernel, (modes, comps, axials, azims, terms, slots)),
        out_shape=jax.ShapeDtypeStruct((vectors, rows, radials), F32),
        in_specs=[anywhere, anywhere, anywhere, scalar, scalar],
        out_specs=anywhere,
        scratch_shapes=[
            pltpu.VMEM((vectors, rows + 2 * PAD, radials), F32),
            pltpu.VMEM((terms, rows, radials), F32),
            pltpu.VMEM((2, vectors, axials, radials), F32),
            pltpu.VMEM((2, vectors, axials, radials), F32),
            pltpu.VMEM((2, vectors // 2, 2 * azims, radials), F32),
            pltpu.VMEM((2, vectors // 2, 2 * azims, radials), F32),
            pltpu.VMEM((16, 2 * vectors, 8, radials), F32),
            pltpu.VMEM((2 * vectors, 8, radials), F32),
            pltpu.VMEM((vectors, rows, radials), F32),
            dma((3,)), dma((4,)), dma((2,)), dma((2,)), dma((2,)), dma((2,)), dma((16,)), dma((16,)),
        ],
        compiler_params=pltpu.CompilerParams(
            collective_id=0, has_side_effects=True, vmem_limit_bytes=32 * 2**20
        ),
    )(
        displacement.reshape(vectors, rows, radials),
        mean_modulus.reshape(1, rows, radials),
        kl_fields.reshape(terms - 1, rows, radials),
        triple_cols.transpose(0, 2, 1),
        triple_vals.transpose(0, 2, 1),
    )
    return result.reshape(displacement.shape)


def solution(mesh):
    return jax.shard_map(
        on_device,
        mesh=mesh,
        in_specs=(
            P("chaos", None, "axial", "azim", None),
            P("axial", "azim", None),
            P(None, "axial", "azim", None),
            P(),
            P(),
        ),
        out_specs=P("chaos", None, "axial", "azim", None),
        check_vma=False,
    )
```

time: 310 us -> 100 us (0.32); the launches traced: 305 us -> 100 us
  waiting for transfers between devices: 129 us -> 0 us
  matrix products: 113 us -> 0 us
  Pallas kernels: 0 us -> 92.9 us
  other arithmetic: 18.5 us -> 0 us
  between operations: 13.8 us -> 0.01 us
  local copies, waits for them, and re-layouts: 20.2 us -> 7.09 us
  starting transfers between devices: 10.8 us -> 0 us
    dot_general x8 -> x0, matrix products: 113 us -> none  [combine(): jnp.einsum('ij,jcazr->icazr', matrices[which], stiffened, precision=lax.P...]
    all_gather x1 -> x0, waiting for transfers between devices: 99.8 us -> none  [on_device(): gathered = lax.all_gather(displacement, 'chaos', axis=0, tiled=True)]
    pallas_call x0 -> x1, Pallas kernels: none -> 92.9 us  [on_device(): pl.pallas_call(functools.partial(kernel, (modes, comps, axials, azims, te...]
    ppermute x4 -> x0, waiting for transfers between devices: 29.2 us -> none  [the longest x2 23.2 us: extended(): lax.ppermute(lax.slice_in_dim(block, 0, width, axis=dim), axis, backward)]
    add x3 -> x0, other arithmetic: 17.2 us -> none  [the longest x1 17.2 us: lame_mix(): weight_axial * dif_axial + weight_azim * dif_azim]
    ppermute x4 -> x0, starting transfers between devices: 10.8 us -> none  [the longest x2 8.07 us: extended(): lax.ppermute(lax.slice_in_dim(block, 0, width, axis=dim), axis, backward)]
    slice x3 -> x0, local copies, waits for them, and re-layouts: 6.81 us -> none  [the longest x2 6.74 us: extended(): lax.slice_in_dim(block, 0, width, axis=dim)]
    add x1 -> x0, local copies, waits for them, and re-layouts: 5.04 us -> none  [combine(): running = scaled if running is None else running + scaled]
  transfers between devices with their start and end apart: 5 -> 0, of which waited for: 5 -> 0; matrix products, arithmetic and copies ran while one was open for 3% -> 0% of each run, Pallas kernels for 0% -> 0%
where the time goes in v1:
time: 100 us
  Pallas kernels  92.9 us (93%)
  local copies, waits for them, and re-layouts  7.09 us (7%)
    pallas_call x1, Pallas kernels, on_device(): pl.pallas_call(functools.partial(kernel, (modes, comps, axials, azims, te...  92.9 us
    unnamed x11, local copies, waits for them, and re-layouts  7.09 us

profile of v1, /device:TPU:1, one launch (start us, length us, event | category | flops | bytes accessed | tf_op | source)
XLA Modules:
  0.0 100.0 jit_solution(9974441821203325070)
XLA Ops:
  0.0 0.0 copy-start
  0.0 2.0 %copy-done = f32[18,3,32,4,128]{4,3,2,1,0:T(4,128)S(1)} copy-done((f32[18,3,32,4,128]{4,3,2,1,0:T(4,128)S(1)}, f32[18,3,32,4,128]{4,3,2,1,0:T(4,128)}, u32[]{:S(2)}) %copy-start) | copy-done | bytes 3538968
  2.0 0.0 copy-start.1
  2.0 1.0 %copy-done.1 = f32[7,32,4,128]{3,2,1,0:T(4,128)S(1)} copy-done((f32[7,32,4,128]{3,2,1,0:T(4,128)S(1)}, f32[7,32,4,128]{3,2,1,0:T(4,128)}, u32[]{:S(2)}) %copy-start.1) | copy-done | bytes 458776
  3.0 0.0 copy-start.2
  3.0 0.8 copy-done.2
  3.9 0.0 copy-start.3
  3.9 0.7 copy-done.3
  4.6 0.0 copy-start.4
  4.6 0.7 copy-done.4
  5.3 92.9 %shard_map.55 = f32[54,128,128]{2,1,0:T(8,128)S(1)} custom-call(f32[54,128,128]{2,1,0:T(8,128)S(1)} %bitcast.7, f32[1,128,128]{2,1,0:T(8,128)S(1)} %bitcast.9, f32[7,128,128]{2,1,0:T(8,128)S(1)} %bitcast.8, s32[8,4,36]{2,1,0:T(4,128)S(1)} %bitcast.10, f32[8,4,36]{2,1,0:T(4,128)S(1)} %bitcast.11), custom_call_target="tpu_custom_call" | custom-call | tf_op jit(solution)/shard_map/pallas_call | solution.py:245
  98.2 1.8 %copy.7 = f32[18,3,32,4,128]{4,3,2,1,0:T(4,128)} copy(f32[18,3,32,4,128]{4,3,2,1,0:T(4,128)S(1)} %bitcast.6) | data formatting | bytes 7077888
Async XLA Ops:
  0.0 2.0 %copy-start = (f32[18,3,32,4,128]{4,3,2,1,0:T(4,128)S(1)}, f32[18,3,32,4,128]{4,3,2,1,0:T(4,128)}, u32[]{:S(2)}) copy-start(f32[18,3,32,4,128]{4,3,2,1,0:T(4,128)} %param.5) | copy-start | bytes 10616836
  2.0 1.0 %copy-start.1 = (f32[7,32,4,128]{3,2,1,0:T(4,128)S(1)}, f32[7,32,4,128]{3,2,1,0:T(4,128)}, u32[]{:S(2)}) copy-start(f32[7,32,4,128]{3,2,1,0:T(4,128)} %param.7) | copy-start | bytes 1376260
  3.0 0.8 copy-start.2
  3.9 0.7 copy-start.3
  4.6 0.7 copy-start.4

commit v2 on v0

v2 whole, which is shorter than its diff:
```python
import functools

import jax
import jax.numpy as jnp
from jax import lax
from jax.experimental import pallas as pl
from jax.experimental.pallas import tpu as pltpu
from jax.sharding import PartitionSpec as P

MESH = pl.DeviceIdType.MESH
F32 = jnp.float32
PAD = 8


def place_of(group, place):
    if group == 0:
        return 1 + place % 2, 1 + place // 2
    if group == 1:
        return 1 + place // 2, 3 * (place % 2)
    return 3 * (place % 2), 2 * (group - 2) + place // 2


LOADS = ((24, 48, 0, 1), (24, 48, 1, 2), (72, 32, 0, 3), (0, 24, 0, 3), (104, 24, 0, 3))


def kernel(
    shape,
    u_hbm, faces_hbm, mean_hbm, kl_hbm, cols_hbm, vals_hbm, out,
    u, fields, cols, vals, azim_send, azim_recv, axial_recv, stiff, work, matrix,
    load_sem, azim_ssem, azim_rsem, axial_ssem, axial_rsem, send_sem, recv_sem, hello,
):
    modes, comps, axials, azims, terms, slots = shape
    rows = axials * azims
    vectors = modes * comps
    last = 15
    chaos = lax.axis_index("chaos")
    azim = lax.axis_index("azim")
    axial = lax.axis_index("axial")
    n_azim, n_axial = lax.axis_size("azim"), lax.axis_size("axial")
    partner = {"chaos": 1 - chaos}
    azim_next = {"azim": lax.rem(azim + 1, n_azim)}
    azim_prev = {"azim": lax.rem(azim + n_azim - 1, n_azim)}
    axial_next = {"axial": lax.rem(axial + 1, n_axial)}
    axial_prev = {"axial": lax.rem(axial + n_axial - 1, n_axial)}
    has_prev, has_next = axial > 0, axial < n_axial - 1
    even = lax.rem(azim, 2) == 0

    barrier = pltpu.get_barrier_semaphore()
    for target in (partner, axial_next, axial_prev):
        pl.semaphore_signal(barrier, inc=1, device_id=target, device_id_type=MESH)

    @pl.when(even)
    def _():
        for target in (azim_next, azim_prev):
            pl.semaphore_signal(barrier, inc=1, device_id=target, device_id_type=MESH)

    loads = [
        pltpu.make_async_copy(
            u_hbm.at[:, pl.ds(c, count_c), pl.ds(first, count)],
            u.at[:, pl.ds(c, count_c), pl.ds(PAD + first, count)],
            load_sem.at[n],
        )
        for n, (first, count, c, count_c) in enumerate(LOADS)
    ]
    later = [
        pltpu.make_async_copy(source, target, load_sem.at[len(LOADS) + n])
        for n, (source, target) in enumerate((
            (mean_hbm, fields.at[pl.ds(0, 1)]),
            (kl_hbm, fields.at[pl.ds(1, terms - 1)]),
            (cols_hbm, cols),
            (vals_hbm, vals),
        ))
    ]
    for copy in loads + later:
        copy.start()

    def remote(source, target, ssem, rsem, device):
        return pltpu.make_async_remote_copy(
            src_ref=source, dst_ref=target, send_sem=ssem, recv_sem=rsem,
            device_id=device, device_id_type=MESH,
        )

    axial_copies = [
        remote(faces_hbm.at[:, :, a], axial_recv.at[s], axial_ssem.at[s], axial_rsem.at[s], d)
        for s, a, d in ((0, 0, axial_prev), (1, axials - 1, axial_next))
    ]
    azim_copies = [
        remote(azim_send.at[s], azim_recv.at[s], azim_ssem.at[s], azim_rsem.at[s], d)
        for s, d in ((0, azim_prev), (1, azim_next))
    ]

    own = pl.ds(chaos * modes, modes)
    first_own, first_other = chaos * modes, (1 - chaos) * modes

    def exchange(n, c):
        part = stiff.at[n, c, own]
        return remote(part, part, send_sem.at[n, c], recv_sem.at[n, c], partner)

    def exchange_block(n):
        part = stiff.at[n, :, own]
        return remote(part, part, send_sem.at[n, 0], recv_sem.at[n, 0], partner)

    lane = lax.broadcasted_iota(jnp.int32, (8, 128), 1)
    first_lane, last_lane = lane == 0, lane == 127

    def stencil(group, places, components):
        def body(j, carry):
            for c in components:
                for place in places:
                    z, at = place_of(group, place)
                    base = PAD + at * 8 * azims + z
                    face = pl.ds(at * 8, 8)

                    def layer(shift):
                        return u[j, c, pl.ds(base + shift, 8, stride=azims), :]

                    x = layer(0)
                    low = layer(-1) if z > 0 else azim_recv[1, j, c, face]
                    high = layer(1) if z < azims - 1 else azim_recv[0, j, c, face]
                    pairs = [
                        layer(azims) + layer(-azims),
                        low + high,
                        jnp.where(first_lane, 0.0, pltpu.roll(x, 1, 1))
                        + jnp.where(last_lane, 0.0, pltpu.roll(x, 127, 1)),
                    ]
                    total = pairs[(c + 1) % 3] + pairs[(c + 2) % 3] + 3.0 * pairs[c]
                    stiff[4 * group + place, c, first_own + j] = 10.0 * x - total
            return carry

        lax.fori_loop(0, modes, body, 0)

    def rows_of(group, place):
        z, at = place_of(group, place)
        return pl.ds(at * (8 * azims) + z, 8, stride=azims)

    def couple(cells, count, put):
        factors = [fields[k, cells, :] for k in range(terms)]

        def row(i, carry):
            mode = first_own + i
            total = [None] * count
            for k in range(terms):
                part = [None] * count
                for s in range(slots):
                    column, value = cols[k, s, mode], vals[k, s, mode]
                    for c in range(count):
                        term = value * work[c, column]
                        part[c] = term if s == 0 else part[c] + term
                for c in range(count):
                    scaled = factors[k] * part[c]
                    total[c] = scaled if k == 0 else total[c] + scaled
            for c in range(count):
                put(i, c, total[c])
            return carry

        lax.fori_loop(0, modes, row, 0)

    def finish(group, first, count, start):
        def block(place, carry):
            n = 4 * group + place
            cells = rows_of(group, place)

            exchange_block(n).wait_send()
            start(place)
            exchange_block(n).wait_recv()

            def gather(j, carry):
                for c in range(comps):
                    work[c, j] = stiff[n, c, j]
                return carry

            lax.fori_loop(0, 2 * modes, gather, 0, unroll=4)

            def put(i, c, value):
                out[i, c, cells, :] = value

            couple(cells, comps, put)
            return carry

        lax.fori_loop(first, first + count, block, 0)

    last_cells = rows_of(3, 3)
    zero = jnp.zeros((8, 128), F32)

    def begin_last():
        def gather(j, carry):
            for c in range(comps):
                work[c, first_own + j] = stiff[last, c, first_own + j]
                work[c, first_other + j] = zero
            return carry

        lax.fori_loop(0, modes, gather, 0, unroll=2)

        def put(i, c, value):
            out[i, c, last_cells, :] = value

        couple(last_cells, comps, put)

    def fill_matrix(first, count):
        def three(q, carry):
            def unit(j, carry):
                for c in range(comps):
                    work[c, j] = jnp.where(j == first_other + q * comps + c, zero + 1.0, zero)
                return carry

            lax.fori_loop(0, 2 * modes, unit, 0, unroll=4)

            def put(i, c, value):
                matrix[i, q * comps + c] = value

            couple(last_cells, comps, put)
            return carry

        lax.fori_loop(first, first + count, three, 0)

    def finish_last():
        def piece(c, carry):
            exchange(last, c).wait_recv()
            values = [stiff[last, c, first_other + j] for j in range(modes)]

            def row(i, carry):
                sums = [out[i, c, last_cells, :], zero, zero]
                for j in range(modes):
                    sums[j % 3] = sums[j % 3] + matrix[i, j] * values[j]
                out[i, c, last_cells, :] = sums[0] + (sums[1] + sums[2])
                return carry

            lax.fori_loop(0, modes, row, 0, unroll=2)
            return carry

        lax.fori_loop(0, comps, piece, 0)

    loads[0].wait()
    stencil(0, (0,), (0,))

    @pl.when(even)
    def _():
        pl.semaphore_wait(barrier, 3)

    @pl.when(jnp.logical_not(even))
    def _():
        pl.semaphore_wait(barrier, 5)

    @pl.when(has_prev)
    def _():
        axial_copies[0].start()

    @pl.when(has_next)
    def _():
        axial_copies[1].start()

    loads[1].wait()
    stencil(0, (0,), (1, 2))
    exchange_block(0).start()
    stencil(0, (1,), (0, 1, 2))
    exchange_block(1).start()

    @pl.when(jnp.logical_not(even))
    def _():
        for target in (azim_next, azim_prev):
            pl.semaphore_signal(hello, inc=1, device_id=target, device_id_type=MESH)

    for copy in loads[2:]:
        copy.wait()

    stencil(0, (2, 3), range(comps))

    for has, s, first in ((has_prev, 1, PAD - azims), (has_next, 0, PAD + rows)):
        @pl.when(has)
        def _(s=s, first=first):
            axial_copies[s].wait_recv()

            def unpack(j, carry):
                for c in range(comps):
                    u[j, c, first:first + azims, :] = axial_recv[s, j, c]
                return carry

            lax.fori_loop(0, modes, unpack, 0)

        @pl.when(jnp.logical_not(has))
        def _(first=first):
            def clear(j, carry):
                for c in range(comps):
                    u[j, c, first:first + azims, :] = jnp.zeros((azims, 128), F32)
                return carry

            lax.fori_loop(0, modes, clear, 0)

    stencil(1, range(4), range(comps))
    for copy in later:
        copy.wait()

    def two_on(group):
        return lambda place: exchange_block(4 * group + place + 2).start()

    finish(0, 0, 1, two_on(0))

    def pack_azim(j, carry):
        for c in range(comps):
            for at in range(axials // 8):
                for s, z in ((0, 0), (1, azims - 1)):
                    azim_send[s, j, c, pl.ds(at * 8, 8)] = u[
                        j, c, pl.ds(PAD + at * 8 * azims + z, 8, stride=azims), :]
        return carry

    lax.fori_loop(0, modes, pack_azim, 0)

    @pl.when(even)
    def _():
        pl.semaphore_wait(hello, 2)

    for copy in azim_copies:
        copy.start()

    finish(0, 1, 3, two_on(0))
    finish(1, 0, 2, two_on(1))
    for copy in azim_copies:
        copy.wait_recv()
    stencil(2, range(4), range(comps))
    stencil(3, range(4), range(comps))
    finish(1, 2, 2, two_on(1))
    begin_last()
    fill_matrix(0, 3)
    finish(2, 0, 4, two_on(2))
    fill_matrix(3, 3)

    def start_few(place):
        @pl.when(place == 0)
        def _():
            exchange_block(14).start()

        @pl.when(place == 2)
        def _():
            for c in range(comps):
                exchange(last, c).start()

    finish(3, 0, 3, start_few)
    finish_last()

    @pl.when(has_prev)
    def _():
        axial_copies[0].wait_send()

    @pl.when(has_next)
    def _():
        axial_copies[1].wait_send()

    for copy in azim_copies:
        copy.wait_send()
    for c in range(comps):
        exchange(last, c).wait_send()


def on_device(displacement, mean_modulus, kl_fields, triple_cols, triple_vals):
    modes, comps, axials, azims, radials = displacement.shape
    terms, all_modes, slots = triple_cols.shape
    rows = axials * azims
    dma = pltpu.SemaphoreType.DMA
    result = pl.pallas_call(
        functools.partial(kernel, (modes, comps, axials, azims, terms, slots)),
        out_shape=jax.ShapeDtypeStruct((modes, comps, rows, radials), F32),
        in_specs=[pl.BlockSpec(memory_space=pltpu.HBM)] * 6,
        out_specs=pl.BlockSpec(memory_space=pltpu.VMEM),
        scratch_shapes=[
            pltpu.VMEM((modes, comps, rows + 2 * PAD, radials), F32),
            pltpu.VMEM((terms, rows, radials), F32),
            pltpu.SMEM((terms, slots, all_modes), jnp.int32),
            pltpu.SMEM((terms, slots, all_modes), F32),
            pltpu.VMEM((2, modes, comps, axials, radials), F32),
            pltpu.VMEM((2, modes, comps, axials, radials), F32),
            pltpu.VMEM((2, modes, comps, azims, radials), F32),
            pltpu.VMEM((16, comps, 2 * modes, 8, radials), F32),
            pltpu.VMEM((comps, 2 * modes, 8, radials), F32),
            pltpu.VMEM((modes, modes, 8, radials), F32),
            dma((len(LOADS) + 4,)), dma((2,)), dma((2,)), dma((2,)), dma((2,)),
            dma((16, comps)), dma((16, comps)), pltpu.SemaphoreType.REGULAR,
        ],
        compiler_params=pltpu.CompilerParams(
            collective_id=0, has_side_effects=True, vmem_limit_bytes=32 * 2**20
        ),
    )(*(
        pltpu.with_memory_space_constraint(x, pltpu.HBM)
        for x in (
            displacement.reshape(modes, comps, rows, radials),
            displacement,
            mean_modulus.reshape(1, rows, radials),
            kl_fields.reshape(terms - 1, rows, radials),
            triple_cols.transpose(0, 2, 1),
            triple_vals.transpose(0, 2, 1),
        )
    ))
    return result.reshape(displacement.shape)


def solution(mesh):
    return jax.shard_map(
        on_device,
        mesh=mesh,
        in_specs=(
            P("chaos", None, "axial", "azim", None),
            P("axial", "azim", None),
            P(None, "axial", "azim", None),
            P(),
            P(),
        ),
        out_specs=P("chaos", None, "axial", "azim", None),
        check_vma=False,
    )
```

time: 310 us -> 87.4 us (0.28)
  the two profiles are of different devices: /device:TPU:1 before, /device:TPU:122 now
where the time goes in v2:
time: 87.4 us; the launch traced here: 87.3 us
  Pallas kernels  85.5 us (98%)
  local copies, waits for them, and re-layouts  1.8 us (2%)
    pallas_call x1, Pallas kernels, on_device(): pl.pallas_call(functools.partial(kernel, (modes, comps, axials, azims, te...  85.5 us
    unnamed x1, local copies, waits for them, and re-layouts  1.8 us

profile of v2, /device:TPU:122, one launch (start us, length us, event | category | flops | bytes accessed | tf_op | source)
XLA Modules:
  0.0 87.3 jit_solution(18242159933191064927)
XLA Ops:
  0.0 85.5 %shard_map.55 = f32[18,3,128,128]{3,2,1,0:T(8,128)S(1)} custom-call(f32[18,3,128,128]{3,2,1,0:T(8,128)} %bitcast.7, f32[18,3,32,4,128]{4,3,2,1,0:T(4,128)} %faces_hbm.1, f32[1,128,128]{2,1,0:T(8,128)} %bitcast.9, f32[7,128,128]{2,1,0:T(8,128)} %bitcast.8, s32[8,4,36]{2,1,0:T(4,128)} %bitcast.10, f32[8,4,36]{2,1,0:T(4,128)} %bitcast.11), custom_call_target="tpu_custom_call" | custom-call | tf_op jit(solution)/shard_map/pallas_call | solution.py:359
  85.5 1.8 %copy.7 = f32[18,3,32,4,128]{4,3,2,1,0:T(4,128)} copy(f32[18,3,32,4,128]{4,3,2,1,0:T(4,128)S(1)} %bitcast.6) | data formatting | bytes 7077888

commit v3 on v2

--- a/solution.py
+++ b/solution.py
@@ -25,9 +25,9 @@
 
 def kernel(
     shape,
-    u_hbm, faces_hbm, mean_hbm, kl_hbm, cols_hbm, vals_hbm, out,
-    u, fields, cols, vals, azim_send, azim_recv, axial_recv, stiff, work, matrix,
-    load_sem, azim_ssem, azim_rsem, axial_ssem, axial_rsem, send_sem, recv_sem, hello,
+    u_hbm, faces_hbm, mean_hbm, kl_hbm, cols_hbm, vals_hbm, out_any,
+    u, fields, cols, vals, azim_send, azim_recv, axial_recv, stiff, work, matrix, out,
+    load_sem, store_sem, azim_ssem, azim_rsem, axial_ssem, axial_rsem, send_sem, recv_sem, hello,
 ):
     modes, comps, axials, azims, terms, slots = shape
     rows = axials * azims
@@ -58,20 +58,20 @@
         pltpu.make_async_copy(
             u_hbm.at[:, pl.ds(c, count_c), pl.ds(first, count)],
             u.at[:, pl.ds(c, count_c), pl.ds(PAD + first, count)],
-            load_sem.at[n],
+            load_sem.at[min(n, 2)],
         )
         for n, (first, count, c, count_c) in enumerate(LOADS)
     ]
     later = [
-        pltpu.make_async_copy(source, target, load_sem.at[len(LOADS) + n])
+        pltpu.make_async_copy(source, target, load_sem.at[max(3, 2 + n)])
         for n, (source, target) in enumerate((
-            (mean_hbm, fields.at[pl.ds(0, 1)]),
-            (kl_hbm, fields.at[pl.ds(1, terms - 1)]),
+            (mean_hbm, fields.at[pl.ds(0, 1), pl.ds(0, rows)]),
+            (kl_hbm, fields.at[pl.ds(1, terms - 1), pl.ds(0, rows)]),
             (cols_hbm, cols),
             (vals_hbm, vals),
         ))
     ]
-    for copy in loads + later:
+    for copy in loads[:3]:
         copy.start()
 
     def remote(source, target, ssem, rsem, device):
@@ -85,7 +85,7 @@
         for s, a, d in ((0, 0, axial_prev), (1, axials - 1, axial_next))
     ]
     azim_copies = [
-        remote(azim_send.at[s], azim_recv.at[s], azim_ssem.at[s], azim_rsem.at[s], d)
+        remote(azim_send.at[s], azim_recv.at[s], azim_ssem, azim_rsem.at[s], d)
         for s, d in ((0, azim_prev), (1, azim_next))
     ]
 
@@ -94,16 +94,16 @@
 
     def exchange(n, c):
         part = stiff.at[n, c, own]
-        return remote(part, part, send_sem.at[n, c], recv_sem.at[n, c], partner)
+        return remote(part, part, send_sem, recv_sem.at[n if n == 0 else n + c], partner)
 
     def exchange_block(n):
         part = stiff.at[n, :, own]
-        return remote(part, part, send_sem.at[n, 0], recv_sem.at[n, 0], partner)
+        return remote(part, part, send_sem, recv_sem.at[n], partner)
 
     lane = lax.broadcasted_iota(jnp.int32, (8, 128), 1)
     first_lane, last_lane = lane == 0, lane == 127
 
-    def stencil(group, places, components):
+    def stencil(group, places, unroll, components=(0, 1, 2)):
         def body(j, carry):
             for c in components:
                 for place in places:
@@ -127,7 +127,7 @@
                     stiff[4 * group + place, c, first_own + j] = 10.0 * x - total
             return carry
 
-        lax.fori_loop(0, modes, body, 0)
+        lax.fori_loop(0, modes, body, 0, unroll=unroll)
 
     def rows_of(group, place):
         z, at = place_of(group, place)
@@ -155,13 +155,11 @@
 
         lax.fori_loop(0, modes, row, 0)
 
-    def finish(group, first, count, start):
+    def finish(group, first, count):
         def block(place, carry):
             n = 4 * group + place
             cells = rows_of(group, place)
 
-            exchange_block(n).wait_send()
-            start(place)
             exchange_block(n).wait_recv()
 
             def gather(j, carry):
@@ -213,6 +211,10 @@
 
         lax.fori_loop(first, first + count, three, 0)
 
+    def store(at, c):
+        part = pl.ds(at * 8 * azims, 8 * azims)
+        return pltpu.make_async_copy(out.at[:, c, part], out_any.at[:, c, part], store_sem)
+
     def finish_last():
         def piece(c, carry):
             exchange(last, c).wait_recv()
@@ -225,13 +227,14 @@
                 out[i, c, last_cells, :] = sums[0] + (sums[1] + sums[2])
                 return carry
 
-            lax.fori_loop(0, modes, row, 0, unroll=2)
+            lax.fori_loop(0, modes, row, 0, unroll=3)
+            store(3, c).start()
             return carry
 
         lax.fori_loop(0, comps, piece, 0)
 
     loads[0].wait()
-    stencil(0, (0,), (0,))
+    stencil(0, (0,), 18, (0,))
 
     @pl.when(even)
     def _():
@@ -249,51 +252,28 @@
     def _():
         axial_copies[1].start()
 
+    for copy in loads[3:] + later:
+        copy.start()
+    exchange(0, 0).start()
     loads[1].wait()
-    stencil(0, (0,), (1, 2))
-    exchange_block(0).start()
-    stencil(0, (1,), (0, 1, 2))
-    exchange_block(1).start()
+    stencil(0, (0,), 9, (1, 2))
+    exchange(0, 1).start()
+    exchange(0, 2).start()
 
     @pl.when(jnp.logical_not(even))
     def _():
         for target in (azim_next, azim_prev):
             pl.semaphore_signal(hello, inc=1, device_id=target, device_id_type=MESH)
 
-    for copy in loads[2:]:
-        copy.wait()
-
-    stencil(0, (2, 3), range(comps))
-
-    for has, s, first in ((has_prev, 1, PAD - azims), (has_next, 0, PAD + rows)):
-        @pl.when(has)
-        def _(s=s, first=first):
-            axial_copies[s].wait_recv()
-
-            def unpack(j, carry):
-                for c in range(comps):
-                    u[j, c, first:first + azims, :] = axial_recv[s, j, c]
-                return carry
-
-            lax.fori_loop(0, modes, unpack, 0)
-
-        @pl.when(jnp.logical_not(has))
-        def _(first=first):
-            def clear(j, carry):
-                for c in range(comps):
-                    u[j, c, first:first + azims, :] = jnp.zeros((azims, 128), F32)
-                return carry
-
-            lax.fori_loop(0, modes, clear, 0)
-
-    stencil(1, range(4), range(comps))
-    for copy in later:
-        copy.wait()
-
-    def two_on(group):
-        return lambda place: exchange_block(4 * group + place + 2).start()
-
-    finish(0, 0, 1, two_on(0))
+    stencil(0, (1,), 6)
+    exchange_block(1).start()
+    rest = sum(count for first, count, c, count_c in LOADS[2:])
+    pltpu.make_async_copy(
+        u_hbm.at[:, :, pl.ds(0, rest)], u.at[:, :, pl.ds(PAD, rest)], load_sem.at[2]
+    ).wait()
+    stencil(0, (2, 3), 3)
+    exchange_block(2).start()
+    exchange_block(3).start()
 
     def pack_azim(j, carry):
         for c in range(comps):
@@ -305,36 +285,66 @@
 
     lax.fori_loop(0, modes, pack_azim, 0)
 
+    for has, s, first in ((has_prev, 1, PAD - azims), (has_next, 0, PAD + rows)):
+        @pl.when(has)
+        def _(s=s, first=first):
+            axial_copies[s].wait_recv()
+
+            def unpack(j, carry):
+                for c in range(comps):
+                    u[j, c, first:first + azims, :] = axial_recv[s, j, c]
+                return carry
+
+            lax.fori_loop(0, modes, unpack, 0, unroll=3)
+
+        @pl.when(jnp.logical_not(has))
+        def _(first=first):
+            def clear(j, carry):
+                for c in range(comps):
+                    u[j, c, first:first + azims, :] = jnp.zeros((azims, 128), F32)
+                return carry
+
+            lax.fori_loop(0, modes, clear, 0, unroll=3)
+
+    stencil(1, range(4), 2)
+    for n in range(4, 8):
+        exchange_block(n).start()
+
     @pl.when(even)
     def _():
         pl.semaphore_wait(hello, 2)
 
     for copy in azim_copies:
         copy.start()
-
-    finish(0, 1, 3, two_on(0))
-    finish(1, 0, 2, two_on(1))
+    whole = fields.at[:, pl.ds(0, rows)]
+    pltpu.make_async_copy(whole, whole, load_sem.at[3]).wait()
+    for copy in later[2:]:
+        copy.wait()
+    finish(0, 0, 4)
+    finish(1, 0, 1)
     for copy in azim_copies:
         copy.wait_recv()
-    stencil(2, range(4), range(comps))
-    stencil(3, range(4), range(comps))
-    finish(1, 2, 2, two_on(1))
+    stencil(2, range(4), 2)
+    for n in range(8, 12):
+        exchange_block(n).start()
+    stencil(3, range(4), 2)
+    for n in range(12, last):
+        exchange_block(n).start()
+    for c in range(comps):
+        exchange(last, c).start()
+    finish(1, 1, 3)
     begin_last()
     fill_matrix(0, 3)
-    finish(2, 0, 4, two_on(2))
+    finish(2, 0, 4)
+    for at in range(2):
+        for c in range(comps):
+            store(at, c).start()
     fill_matrix(3, 3)
 
-    def start_few(place):
-        @pl.when(place == 0)
-        def _():
-            exchange_block(14).start()
-
-        @pl.when(place == 2)
-        def _():
-            for c in range(comps):
-                exchange(last, c).start()
-
-    finish(3, 0, 3, start_few)
+    finish(3, 0, 2)
+    for c in range(comps):
+        store(2, c).start()
+    finish(3, 2, 1)
     finish_last()
 
     @pl.when(has_prev)
@@ -345,10 +355,10 @@
     def _():
         axial_copies[1].wait_send()
 
-    for copy in azim_copies:
-        copy.wait_send()
-    for c in range(comps):
-        exchange(last, c).wait_send()
+    remote(azim_send, azim_recv, azim_ssem, azim_rsem.at[0], azim_next).wait_send()
+    every = stiff.at[:, :, own]
+    remote(every, every, send_sem, recv_sem.at[0], partner).wait_send()
+    pltpu.make_async_copy(out.at[:, :, pl.ds(0, rows)], out_any, store_sem).wait()
 
 
 def on_device(displacement, mean_modulus, kl_fields, triple_cols, triple_vals):
@@ -360,10 +370,10 @@
         functools.partial(kernel, (modes, comps, axials, azims, terms, slots)),
         out_shape=jax.ShapeDtypeStruct((modes, comps, rows, radials), F32),
         in_specs=[pl.BlockSpec(memory_space=pltpu.HBM)] * 6,
-        out_specs=pl.BlockSpec(memory_space=pltpu.VMEM),
+        out_specs=pl.BlockSpec(memory_space=pl.ANY),
         scratch_shapes=[
             pltpu.VMEM((modes, comps, rows + 2 * PAD, radials), F32),
-            pltpu.VMEM((terms, rows, radials), F32),
+            pltpu.VMEM((terms, rows + PAD, radials), F32),
             pltpu.SMEM((terms, slots, all_modes), jnp.int32),
             pltpu.SMEM((terms, slots, all_modes), F32),
             pltpu.VMEM((2, modes, comps, axials, radials), F32),
@@ -372,8 +382,9 @@
             pltpu.VMEM((16, comps, 2 * modes, 8, radials), F32),
             pltpu.VMEM((comps, 2 * modes, 8, radials), F32),
             pltpu.VMEM((modes, modes, 8, radials), F32),
-            dma((len(LOADS) + 4,)), dma((2,)), dma((2,)), dma((2,)), dma((2,)),
-            dma((16, comps)), dma((16, comps)), pltpu.SemaphoreType.REGULAR,
+            pltpu.VMEM((modes, comps, rows + PAD, radials), F32),
+            dma((6,)), dma(()), dma(()), dma((2,)), dma((2,)), dma((2,)),
+            dma(()), dma((18,)), pltpu.SemaphoreType.REGULAR,
         ],
         compiler_params=pltpu.CompilerParams(
             collective_id=0, has_side_effects=True, vmem_limit_bytes=32 * 2**20

time: 87.4 us -> 85.9 us (0.983)
  the two profiles are of different devices: /device:TPU:122 before, /device:TPU:1 now
where the time goes in v3:
time: 85.9 us; the launch traced here: 85.5 us
  Pallas kernels  83.7 us (97%)
  local copies, waits for them, and re-layouts  1.8 us (2%)
    pallas_call x1, Pallas kernels, on_device(): pl.pallas_call(functools.partial(kernel, (modes, comps, axials, azims, te...  83.7 us
    unnamed x1, local copies, waits for them, and re-layouts  1.8 us

profile of v3, /device:TPU:1, one launch (start us, length us, event | category | flops | bytes accessed | tf_op | source)
XLA Modules:
  0.0 85.5 jit_solution(11977686814139386351)
XLA Ops:
  0.0 83.7 %shard_map.55 = f32[18,3,128,128]{3,2,1,0:T(8,128)S(1)} custom-call(f32[18,3,128,128]{3,2,1,0:T(8,128)} %bitcast.7, f32[18,3,32,4,128]{4,3,2,1,0:T(4,128)} %faces_hbm.1, f32[1,128,128]{2,1,0:T(8,128)} %bitcast.9, f32[7,128,128]{2,1,0:T(8,128)} %bitcast.8, s32[8,4,36]{2,1,0:T(4,128)} %bitcast.10, f32[8,4,36]{2,1,0:T(4,128)} %bitcast.11), custom_call_target="tpu_custom_call" | custom-call | tf_op jit(solution)/shard_map/pallas_call | solution.py:369
  83.7 1.8 %copy.7 = f32[18,3,32,4,128]{4,3,2,1,0:T(4,128)} copy(f32[18,3,32,4,128]{4,3,2,1,0:T(4,128)S(1)} %bitcast.6) | data formatting | bytes 7077888

commit v4 on v3

--- a/solution.py
+++ b/solution.py
@@ -20,7 +20,12 @@
     return 3 * (place % 2), 2 * (group - 2) + place // 2
 
 
-LOADS = ((24, 48, 0, 1), (24, 48, 1, 2), (72, 32, 0, 3), (0, 24, 0, 3), (104, 24, 0, 3))
+FEW = 6
+TAIL = ((0, 9), (9, 6), (15, 3))
+LOADS = (
+    (0, FEW, 0, 1, 24, 48), (FEW, 12, 0, 1, 24, 48), (0, 18, 1, 2, 24, 48),
+    (0, 18, 0, 3, 72, 32), (0, 18, 0, 3, 0, 24), (0, 18, 0, 3, 104, 24),
+)
 
 
 def kernel(
@@ -45,6 +50,16 @@
     has_prev, has_next = axial > 0, axial < n_axial - 1
     even = lax.rem(azim, 2) == 0
 
+    loads = [
+        pltpu.make_async_copy(
+            u_hbm.at[pl.ds(j, count_j), pl.ds(c, count_c), pl.ds(first, count)],
+            u.at[pl.ds(j, count_j), pl.ds(c, count_c), pl.ds(PAD + first, count)],
+            load_sem.at[min(n, 3)],
+        )
+        for n, (j, count_j, c, count_c, first, count) in enumerate(LOADS)
+    ]
+    loads[0].start()
+
     barrier = pltpu.get_barrier_semaphore()
     for target in (partner, axial_next, axial_prev):
         pl.semaphore_signal(barrier, inc=1, device_id=target, device_id_type=MESH)
@@ -54,16 +69,8 @@
         for target in (azim_next, azim_prev):
             pl.semaphore_signal(barrier, inc=1, device_id=target, device_id_type=MESH)
 
-    loads = [
-        pltpu.make_async_copy(
-            u_hbm.at[:, pl.ds(c, count_c), pl.ds(first, count)],
-            u.at[:, pl.ds(c, count_c), pl.ds(PAD + first, count)],
-            load_sem.at[min(n, 2)],
-        )
-        for n, (first, count, c, count_c) in enumerate(LOADS)
-    ]
     later = [
-        pltpu.make_async_copy(source, target, load_sem.at[max(3, 2 + n)])
+        pltpu.make_async_copy(source, target, load_sem.at[max(4, 3 + n)])
         for n, (source, target) in enumerate((
             (mean_hbm, fields.at[pl.ds(0, 1), pl.ds(0, rows)]),
             (kl_hbm, fields.at[pl.ds(1, terms - 1), pl.ds(0, rows)]),
@@ -71,7 +78,7 @@
             (vals_hbm, vals),
         ))
     ]
-    for copy in loads[:3]:
+    for copy in loads[1:4]:
         copy.start()
 
     def remote(source, target, ssem, rsem, device):
@@ -89,21 +96,27 @@
         for s, d in ((0, azim_prev), (1, azim_next))
     ]
 
-    own = pl.ds(chaos * modes, modes)
     first_own, first_other = chaos * modes, (1 - chaos) * modes
 
     def exchange(n, c):
-        part = stiff.at[n, c, own]
+        part = stiff.at[n, chaos, c]
         return remote(part, part, send_sem, recv_sem.at[n if n == 0 else n + c], partner)
 
+    def exchange_some(n, c, j, count, sem):
+        part = stiff.at[n, chaos, c, pl.ds(j, count)]
+        return remote(part, part, send_sem, recv_sem.at[sem], partner)
+
+    def exchange_tail(n):
+        return exchange_some(last, comps - 1, *TAIL[n], last + comps - 1 + n)
+
     def exchange_block(n):
-        part = stiff.at[n, :, own]
+        part = stiff.at[n, chaos]
         return remote(part, part, send_sem, recv_sem.at[n], partner)
 
     lane = lax.broadcasted_iota(jnp.int32, (8, 128), 1)
     first_lane, last_lane = lane == 0, lane == 127
 
-    def stencil(group, places, unroll, components=(0, 1, 2)):
+    def stencil(group, places, unroll, components=(0, 1, 2), span=(0, modes)):
         def body(j, carry):
             for c in components:
                 for place in places:
@@ -124,10 +137,10 @@
                         + jnp.where(last_lane, 0.0, pltpu.roll(x, 127, 1)),
                     ]
                     total = pairs[(c + 1) % 3] + pairs[(c + 2) % 3] + 3.0 * pairs[c]
-                    stiff[4 * group + place, c, first_own + j] = 10.0 * x - total
-            return carry
-
-        lax.fori_loop(0, modes, body, 0, unroll=unroll)
+                    stiff[4 * group + place, chaos, c, j] = 10.0 * x - total
+            return carry
+
+        lax.fori_loop(*span, body, 0, unroll=unroll)
 
     def rows_of(group, place):
         z, at = place_of(group, place)
@@ -163,11 +176,12 @@
             exchange_block(n).wait_recv()
 
             def gather(j, carry):
-                for c in range(comps):
-                    work[c, j] = stiff[n, c, j]
+                for half in range(2):
+                    for c in range(comps):
+                        work[c, half * modes + j] = stiff[n, half, c, j]
                 return carry
 
-            lax.fori_loop(0, 2 * modes, gather, 0, unroll=4)
+            lax.fori_loop(0, modes, gather, 0, unroll=3)
 
             def put(i, c, value):
                 out[i, c, cells, :] = value
@@ -183,7 +197,7 @@
     def begin_last():
         def gather(j, carry):
             for c in range(comps):
-                work[c, first_own + j] = stiff[last, c, first_own + j]
+                work[c, first_own + j] = stiff[last, chaos, c, j]
                 work[c, first_other + j] = zero
             return carry
 
@@ -216,46 +230,55 @@
         return pltpu.make_async_copy(out.at[:, c, part], out_any.at[:, c, part], store_sem)
 
     def finish_last():
+        def take(c, first, count, unroll):
+            values = [stiff[last, 1 - chaos, c, first + j] for j in range(count)]
+
+            def row(i, carry):
+                sums = [out[i, c, last_cells, :], zero, zero]
+                for j in range(count):
+                    sums[j % 3] = sums[j % 3] + matrix[i, first + j] * values[j]
+                out[i, c, last_cells, :] = sums[0] + (sums[1] + sums[2])
+                return carry
+
+            lax.fori_loop(0, modes, row, 0, unroll=unroll)
+
         def piece(c, carry):
             exchange(last, c).wait_recv()
-            values = [stiff[last, c, first_other + j] for j in range(modes)]
-
-            def row(i, carry):
-                sums = [out[i, c, last_cells, :], zero, zero]
-                for j in range(modes):
-                    sums[j % 3] = sums[j % 3] + matrix[i, j] * values[j]
-                out[i, c, last_cells, :] = sums[0] + (sums[1] + sums[2])
-                return carry
-
-            lax.fori_loop(0, modes, row, 0, unroll=3)
+            take(c, 0, modes, 3)
             store(3, c).start()
             return carry
 
-        lax.fori_loop(0, comps, piece, 0)
-
+        lax.fori_loop(0, comps - 1, piece, 0)
+        for n, (first, count) in enumerate(TAIL):
+            exchange_tail(n).wait_recv()
+            take(comps - 1, first, count, 18 // count)
+        store(3, comps - 1).start()
+
+    @pl.when(even)
+    def _():
+        pl.semaphore_wait(barrier, 3)
+
+    @pl.when(jnp.logical_not(even))
+    def _():
+        pl.semaphore_wait(barrier, 5)
+
+    @pl.when(has_prev)
+    def _():
+        axial_copies[0].start()
+
+    @pl.when(has_next)
+    def _():
+        axial_copies[1].start()
+
+    for copy in loads[4:] + later:
+        copy.start()
     loads[0].wait()
-    stencil(0, (0,), 18, (0,))
-
-    @pl.when(even)
-    def _():
-        pl.semaphore_wait(barrier, 3)
-
-    @pl.when(jnp.logical_not(even))
-    def _():
-        pl.semaphore_wait(barrier, 5)
-
-    @pl.when(has_prev)
-    def _():
-        axial_copies[0].start()
-
-    @pl.when(has_next)
-    def _():
-        axial_copies[1].start()
-
-    for copy in loads[3:] + later:
-        copy.start()
-    exchange(0, 0).start()
+    stencil(0, (0,), FEW, (0,), (0, FEW))
+    exchange_some(0, 0, 0, FEW, 0).start()
     loads[1].wait()
+    stencil(0, (0,), modes - FEW, (0,), (FEW, modes))
+    exchange_some(0, 0, FEW, modes - FEW, 0).start()
+    loads[2].wait()
     stencil(0, (0,), 9, (1, 2))
     exchange(0, 1).start()
     exchange(0, 2).start()
@@ -267,9 +290,9 @@
 
     stencil(0, (1,), 6)
     exchange_block(1).start()
-    rest = sum(count for first, count, c, count_c in LOADS[2:])
+    rest = sum(load[-1] for load in LOADS[3:])
     pltpu.make_async_copy(
-        u_hbm.at[:, :, pl.ds(0, rest)], u.at[:, :, pl.ds(PAD, rest)], load_sem.at[2]
+        u_hbm.at[:, :, pl.ds(0, rest)], u.at[:, :, pl.ds(PAD, rest)], load_sem.at[3]
     ).wait()
     stencil(0, (2, 3), 3)
     exchange_block(2).start()
@@ -317,7 +340,7 @@
     for copy in azim_copies:
         copy.start()
     whole = fields.at[:, pl.ds(0, rows)]
-    pltpu.make_async_copy(whole, whole, load_sem.at[3]).wait()
+    pltpu.make_async_copy(whole, whole, load_sem.at[4]).wait()
     for copy in later[2:]:
         copy.wait()
     finish(0, 0, 4)
@@ -330,8 +353,10 @@
     stencil(3, range(4), 2)
     for n in range(12, last):
         exchange_block(n).start()
-    for c in range(comps):
+    for c in range(comps - 1):
         exchange(last, c).start()
+    for n in range(len(TAIL)):
+        exchange_tail(n).start()
     finish(1, 1, 3)
     begin_last()
     fill_matrix(0, 3)
@@ -356,7 +381,7 @@
         axial_copies[1].wait_send()
 
     remote(azim_send, azim_recv, azim_ssem, azim_rsem.at[0], azim_next).wait_send()
-    every = stiff.at[:, :, own]
+    every = stiff.at[:, chaos]
     remote(every, every, send_sem, recv_sem.at[0], partner).wait_send()
     pltpu.make_async_copy(out.at[:, :, pl.ds(0, rows)], out_any, store_sem).wait()
 
@@ -379,12 +404,12 @@
             pltpu.VMEM((2, modes, comps, axials, radials), F32),
             pltpu.VMEM((2, modes, comps, axials, radials), F32),
             pltpu.VMEM((2, modes, comps, azims, radials), F32),
-            pltpu.VMEM((16, comps, 2 * modes, 8, radials), F32),
+            pltpu.VMEM((16, 2, comps, modes, 8, radials), F32),
             pltpu.VMEM((comps, 2 * modes, 8, radials), F32),
             pltpu.VMEM((modes, modes, 8, radials), F32),
             pltpu.VMEM((modes, comps, rows + PAD, radials), F32),
-            dma((6,)), dma(()), dma(()), dma((2,)), dma((2,)), dma((2,)),
-            dma(()), dma((18,)), pltpu.SemaphoreType.REGULAR,
+            dma((7,)), dma(()), dma(()), dma((2,)), dma((2,)), dma((2,)),
+            dma(()), dma((20,)), pltpu.SemaphoreType.REGULAR,
         ],
         compiler_params=pltpu.CompilerParams(
             collective_id=0, has_side_effects=True, vmem_limit_bytes=32 * 2**20

time: 85.9 us -> 85.9 us (level)
  no operation moved by 1% of the time
where the time goes in v4:
time: 85.9 us; the launch traced here: 85.3 us
  Pallas kernels  83.5 us (97%)
  local copies, waits for them, and re-layouts  1.8 us (2%)
    pallas_call x1, Pallas kernels, on_device(): pl.pallas_call(functools.partial(kernel, (modes, comps, axials, azims, te...  83.5 us
    unnamed x1, local copies, waits for them, and re-layouts  1.8 us

profile of v4, /device:TPU:1, one launch (start us, length us, event | category | flops | bytes accessed | tf_op | source)
XLA Modules:
  0.0 85.3 jit_solution(1289962195050101973)
XLA Ops:
  0.0 83.5 %shard_map.55 = f32[18,3,128,128]{3,2,1,0:T(8,128)S(1)} custom-call(f32[18,3,128,128]{3,2,1,0:T(8,128)} %bitcast.7, f32[18,3,32,4,128]{4,3,2,1,0:T(4,128)} %faces_hbm.1, f32[1,128,128]{2,1,0:T(8,128)} %bitcast.9, f32[7,128,128]{2,1,0:T(8,128)} %bitcast.8, s32[8,4,36]{2,1,0:T(4,128)} %bitcast.10, f32[8,4,36]{2,1,0:T(4,128)} %bitcast.11), custom_call_target="tpu_custom_call" | custom-call | tf_op jit(solution)/shard_map/pallas_call | solution.py:394
  83.6 1.8 %copy.7 = f32[18,3,32,4,128]{4,3,2,1,0:T(4,128)} copy(f32[18,3,32,4,128]{4,3,2,1,0:T(4,128)S(1)} %bitcast.6) | data formatting | bytes 7077888

commit v5 on v4

--- a/solution.py
+++ b/solution.py
@@ -49,6 +49,12 @@
     axial_prev = {"axial": lax.rem(axial + n_axial - 1, n_axial)}
     has_prev, has_next = axial > 0, axial < n_axial - 1
     even = lax.rem(azim, 2) == 0
+    odd = jnp.logical_not(even)
+    half = n_azim // 2
+    second = chaos == 1
+    cut_before = jnp.logical_and(second, azim == half - 1)
+    cut_after = jnp.logical_and(second, azim == half)
+    relays = jnp.logical_and(chaos == 0, azim == half)
 
     loads = [
         pltpu.make_async_copy(
@@ -66,8 +72,11 @@
 
     @pl.when(even)
     def _():
-        for target in (azim_next, azim_prev):
-            pl.semaphore_signal(barrier, inc=1, device_id=target, device_id_type=MESH)
+        pl.semaphore_signal(barrier, inc=1, device_id=azim_next, device_id_type=MESH)
+
+    @pl.when(jnp.logical_and(even, jnp.logical_not(cut_after)))
+    def _():
+        pl.semaphore_signal(barrier, inc=1, device_id=azim_prev, device_id_type=MESH)
 
     later = [
         pltpu.make_async_copy(source, target, load_sem.at[max(4, 3 + n)])
@@ -258,9 +267,13 @@
     def _():
         pl.semaphore_wait(barrier, 3)
 
-    @pl.when(jnp.logical_not(even))
+    @pl.when(jnp.logical_and(odd, jnp.logical_not(cut_before)))
     def _():
         pl.semaphore_wait(barrier, 5)
+
+    @pl.when(cut_before)
+    def _():
+        pl.semaphore_wait(barrier, 4)
 
     @pl.when(has_prev)
     def _():
@@ -283,10 +296,13 @@
     exchange(0, 1).start()
     exchange(0, 2).start()
 
-    @pl.when(jnp.logical_not(even))
-    def _():
-        for target in (azim_next, azim_prev):
-            pl.semaphore_signal(hello, inc=1, device_id=target, device_id_type=MESH)
+    @pl.when(odd)
+    def _():
+        pl.semaphore_signal(hello, inc=1, device_id=azim_prev, device_id_type=MESH)
+
+    @pl.when(jnp.logical_and(odd, jnp.logical_not(cut_before)))
+    def _():
+        pl.semaphore_signal(hello, inc=1, device_id=azim_next, device_id_type=MESH)
 
     stencil(0, (1,), 6)
     exchange_block(1).start()
@@ -336,6 +352,15 @@
     @pl.when(even)
     def _():
         pl.semaphore_wait(hello, 2)
+
+    @pl.when(relays)
+    def _():
+        for target in (partner, {**partner, **azim_prev}):
+            pl.semaphore_signal(hello, inc=1, device_id=target, device_id_type=MESH)
+
+    @pl.when(cut_before)
+    def _():
+        pl.semaphore_wait(hello, 1)
 
     for copy in azim_copies:
         copy.start()

time: 85.9 us -> 85.5 us (level)
  no operation moved by 1% of the time
where the time goes in v5:
time: 85.5 us; the launch traced here: 85.3 us
  Pallas kernels  83.5 us (98%)
  local copies, waits for them, and re-layouts  1.8 us (2%)
    pallas_call x1, Pallas kernels, on_device(): pl.pallas_call(functools.partial(kernel, (modes, comps, axials, azims, te...  83.5 us
    unnamed x1, local copies, waits for them, and re-layouts  1.8 us

profile of v5, /device:TPU:1, one launch (start us, length us, event | category | flops | bytes accessed | tf_op | source)
XLA Modules:
  0.0 85.3 jit_solution(15521953996783523203)
XLA Ops:
  0.0 83.5 %shard_map.55 = f32[18,3,128,128]{3,2,1,0:T(8,128)S(1)} custom-call(f32[18,3,128,128]{3,2,1,0:T(8,128)} %bitcast.7, f32[18,3,32,4,128]{4,3,2,1,0:T(4,128)} %faces_hbm.1, f32[1,128,128]{2,1,0:T(8,128)} %bitcast.9, f32[7,128,128]{2,1,0:T(8,128)} %bitcast.8, s32[8,4,36]{2,1,0:T(4,128)} %bitcast.10, f32[8,4,36]{2,1,0:T(4,128)} %bitcast.11), custom_call_target="tpu_custom_call" | custom-call | tf_op jit(solution)/shard_map/pallas_call | solution.py:419
  83.6 1.8 %copy.7 = f32[18,3,32,4,128]{4,3,2,1,0:T(4,128)} copy(f32[18,3,32,4,128]{4,3,2,1,0:T(4,128)S(1)} %bitcast.6) | data formatting | bytes 7077888
